TPU v7x, 32 devices: a whole 2x2x4 slice. The times are simulated.
32 devices in a mesh: tm: 16 (over z, x, core), mp: 2 (over y).
Axes of the slice: x: 2, y: 2, z: 4, core: 2. Of those that a mesh axis runs over, the one named last changes fastest.
Arguments:
- tokens: bfloat16 [4096, 1024], P('tm'), may hold values from -9 to 9
- norm1_gain: float32 [1024], replicated, may hold values from 0.5 to 1.5
- query_weight: bfloat16 [1024, 1024], P(None, 'mp'), may hold values from -1 to 1
- key_weight: bfloat16 [1024, 1024], P(None, 'mp'), may hold values from -1 to 1
- value_weight: bfloat16 [1024, 1024], P(None, 'mp'), may hold values from -0.1875 to 0.1875
- output_weight: bfloat16 [1024, 1024], P('mp'), may hold values from -5 to 5
- pattern: int32 [32, 8], replicated, may hold values from -1 to 31, as said below
- adjacency: int32 [128, 128], replicated, may hold values 0 or 1
- decay_rate: float32 [1024], P('mp'), may hold values from 0.015625 to 0.1
- norm2_gain: float32 [1024], replicated, may hold values from 0.5 to 1.5
- up_weight: bfloat16 [1024, 4096], P(None, 'mp'), may hold values from -0.1875 to 0.1875
- down_weight: bfloat16 [4096, 1024], P('mp'), may hold values from -0.09375 to 0.09375
Outputs:
- layer_out: bfloat16 [4096, 1024], P('tm', 'mp')
Inputs may be any that keep to these rules, and one draw needn't show every extreme that they name: pattern[b, 0] = b and pattern[b, 1] = b - 1. For the rows of the blocks g * 2 to g * 2 + 1, entry 2 + k (k from 0 to 5) is the same in all these rows: -1 where g < 2^k, else one of the blocks (g - 2^k) * 2 to (g - 2^k) * 2 + 1, never the block g * 2 - 1.
All inputs are finite; a program needn't handle non-finite values.
Results may differ from a plain program's by a relative error of at most 0.01.
Values may be sent and summed in bfloat16 or wider, within the bound.
A program may use at most 64 MiB of HBM per device.

v0:
```python
import math
import jax
import jax.numpy as jnp
from jax import lax
from jax.sharding import PartitionSpec as P

HD = 128


def from_behind(value, axis, steps):
    count = lax.axis_size(axis)
    first, last = (max(0, -steps), min(count, count - steps))
    return lax.ppermute(value, axis, [(source, source + steps) for source in range(first, last)])


def rms_norm(rows, gain):
    widened = rows.astype(jnp.float32)
    square = jnp.mean(widened * widened, axis=-1, keepdims=True)
    return (widened * lax.rsqrt(square + 1e-05) * gain).astype(jnp.bfloat16)


def block_partial(queries, key_rows, value_rows, heads):
    head_size = queries.shape[-1] // heads
    query_split = queries.reshape(queries.shape[:-1] + (heads, head_size))
    key_split = key_rows.reshape(key_rows.shape[:-1] + (heads, head_size))
    value_split = value_rows.reshape(value_rows.shape[:-1] + (heads, head_size))
    scores = jnp.einsum(
        "...qhd,...khd->...hqk", query_split, key_split, preferred_element_type=jnp.float32
    ) * (1.0 / math.sqrt(head_size))
    tops = jnp.max(scores, axis=-1)
    probs = jnp.exp(scores - tops[..., None])
    totals = jnp.sum(probs, axis=-1)
    weights = probs.astype(jnp.bfloat16)
    outputs = jnp.einsum(
        "...hqk,...khd->...qhd", weights, value_split, preferred_element_type=jnp.float32
    )
    return (tops, totals, outputs.reshape(outputs.shape[:-2] + (heads * head_size,)))


def merge_partials(tops, totals, outputs, valid, heads):
    flags = valid[..., None, None]
    masked = jnp.where(flags, tops, -jnp.inf)
    largest = jnp.max(masked, axis=-3)
    factor = jnp.where(flags, jnp.exp(jnp.where(flags, tops, 0.0) - largest[..., None, :, :]), 0.0)
    denom = jnp.sum(factor * totals, axis=-3)
    split = outputs.reshape(outputs.shape[:-1] + (heads, -1))
    numer = jnp.sum(jnp.swapaxes(factor, -1, -2)[..., None] * split, axis=-4)
    result = numer / jnp.swapaxes(denom, -1, -2)[..., None]
    return result.reshape(result.shape[:-2] + (-1,)).astype(jnp.bfloat16)


def running(frames, retain, inject):
    driven = frames.astype(jnp.float32) * inject
    factors = jnp.broadcast_to(retain, driven.shape)

    def join(earlier, later):
        return (earlier[0] * later[0], later[0] * earlier[1] + later[1])

    return lax.associative_scan(join, (factors, driven), axis=0)[1]


def per_device(
    tokens,
    norm1_gain,
    query_weight,
    key_weight,
    value_weight,
    output_weight,
    pattern,
    adjacency,
    decay_rate,
    norm2_gain,
    up_weight,
    down_weight,
):
    groups = lax.axis_size("tm")
    position = lax.axis_index("tm")
    width = query_weight.shape[1]
    heads = width // HD
    sites = adjacency.shape[0]
    steps = tokens.shape[0] // sites
    normed = rms_norm(tokens, norm1_gain)
    queries = (
        jnp.dot(normed, query_weight, preferred_element_type=jnp.float32)
        .astype(jnp.bfloat16)
        .reshape(steps, sites, width)
    )
    key_rows = jnp.dot(normed, key_weight, preferred_element_type=jnp.float32).astype(jnp.bfloat16)
    value_rows = jnp.dot(normed, value_weight, preferred_element_type=jnp.float32).astype(
        jnp.bfloat16
    )
    key_blocks = key_rows.reshape(steps, sites, width)
    value_blocks = value_rows.reshape(steps, sites, width)
    own_entries = lax.dynamic_slice_in_dim(pattern, position * steps, steps, 0)
    remote = own_entries[:, 2:]
    far_count = remote.shape[1]
    key_last, value_last = from_behind((key_blocks[steps - 1], value_blocks[steps - 1]), "tm", 1)
    prior_keys = jnp.concatenate([key_last[None], key_blocks[:-1]], axis=0)
    prior_values = jnp.concatenate([value_last[None], value_blocks[:-1]], axis=0)
    self_part = block_partial(queries, key_blocks, value_blocks, heads)
    prior_part = block_partial(queries, prior_keys, prior_values, heads)
    spread_queries = jnp.broadcast_to(queries[:, None], (steps, far_count, sites, width))
    wanted = pattern[:, 2:].reshape(groups, -1)
    local_pick = wanted - position * steps
    hits = (wanted >= 0) & (local_pick >= 0) & (local_pick < steps)
    selector = jnp.any(
        (local_pick[:, :, None] == jnp.arange(steps, dtype=jnp.int32)[None, None, :])
        & hits[:, :, None],
        axis=1,
    ).astype(jnp.bfloat16)
    send_keys = jnp.einsum(
        "gs,sbf->gbf", selector, key_blocks, preferred_element_type=jnp.float32
    ).astype(jnp.bfloat16)
    send_values = jnp.einsum(
        "gs,sbf->gbf", selector, value_blocks, preferred_element_type=jnp.float32
    ).astype(jnp.bfloat16)
    got_keys, got_values = (
        lax.all_to_all(send_keys, "tm", split_axis=0, concat_axis=0, tiled=True),
        lax.all_to_all(send_values, "tm", split_axis=0, concat_axis=0, tiled=True),
    )
    source = jnp.maximum(remote, 0) // steps
    far_part = block_partial(spread_queries, got_keys[source], got_values[source], heads)
    tops = jnp.concatenate([self_part[0][:, None], prior_part[0][:, None], far_part[0]], axis=1)
    totals = jnp.concatenate([self_part[1][:, None], prior_part[1][:, None], far_part[1]], axis=1)
    outputs = jnp.concatenate([self_part[2][:, None], prior_part[2][:, None], far_part[2]], axis=1)
    block_ids = position * steps + jnp.arange(steps, dtype=jnp.int32)
    valid = jnp.concatenate(
        [jnp.ones((steps, 1), bool), (block_ids > 0)[:, None], remote >= 0], axis=1
    )
    attended = merge_partials(tops, totals, outputs, valid, heads).reshape(steps * sites, width)
    projected = lax.psum_scatter(
        jnp.dot(attended, output_weight, preferred_element_type=jnp.float32),
        "mp",
        scatter_dimension=1,
        tiled=True,
    )
    columns = projected.shape[1]
    own_tokens = lax.dynamic_slice_in_dim(tokens, lax.axis_index("mp") * columns, columns, 1)
    first = (own_tokens.astype(jnp.float32) + projected).astype(jnp.bfloat16)
    links = jnp.maximum(adjacency, jnp.eye(sites, dtype=jnp.int32))
    degree = jnp.sum(links, axis=1).astype(jnp.float32)
    grid = first.reshape(steps, sites, columns)
    mixed = (
        jnp.einsum(
            "st,btc->bsc", links.astype(jnp.bfloat16), grid, preferred_element_type=jnp.float32
        )
        / degree[None, :, None]
    ).astype(jnp.bfloat16)
    retain = jnp.exp(-decay_rate)
    inject = jnp.sqrt(1.0 - retain * retain)
    by_site = lax.all_to_all(mixed, "tm", split_axis=1, concat_axis=0, tiled=True)
    states = running(by_site, retain, inject).astype(jnp.bfloat16)
    smoothed = lax.all_to_all(states, "tm", split_axis=0, concat_axis=1, tiled=True)
    second = (
        first.astype(jnp.float32) + smoothed.reshape(steps * sites, columns).astype(jnp.float32)
    ).astype(jnp.bfloat16)
    whole = lax.all_gather(second, "mp", axis=1, tiled=True)
    normed_late = rms_norm(whole, norm2_gain)
    hidden = jax.nn.gelu(
        jnp.dot(normed_late, up_weight, preferred_element_type=jnp.float32), approximate=True
    ).astype(jnp.bfloat16)
    summed = lax.psum_scatter(
        jnp.dot(hidden, down_weight, preferred_element_type=jnp.float32),
        "mp",
        scatter_dimension=1,
        tiled=True,
    )
    return (second.astype(jnp.float32) + summed).astype(jnp.bfloat16)


def solution(mesh):
    placed = (
        P("tm", None),
        P(),
        P(None, "mp"),
        P(None, "mp"),
        P(None, "mp"),
        P("mp", None),
        P(),
        P(),
        P("mp"),
        P(),
        P(None, "mp"),
        P("mp", None),
    )
    return jax.shard_map(
        per_device, mesh=mesh, in_specs=placed, out_specs=P("tm", "mp"), check_vma=False
    )
```

profile of v0, /device:TPU:0, one launch (start us, length us, event | category | flops | bytes accessed | tf_op | source)
XLA Modules:
  0.0 243.4 jit_solution(6739945608081619143)
XLA Ops:
  6.5 1.3 fusion.16
  7.9 0.7 slice_compare_fusion
  8.6 0.7 slice_subtract_fusion
  9.4 0.1 copy.136
  9.6 0.1 fusion.75
  9.7 1.9 convolution_convert_fusion.2
  11.6 0.8 convolution_convert_fusion
  12.4 2.5 %copy.148 = bf16[16,128,512]{2,1,0:T(8,128)(2,1)} copy(bf16[16,128,512]{2,0,1:T(8,128)(2,1)S(1)} %convolution_convert_fusion) | data formatting | bytes 4194304 | tf_op jit(solution)/shard_map/convert_element_type | solution.py:116
  15.0 7.5 %all-to-all-start.1 = ((bf16[16,128,512]{2,1,0:T(8,128)(2,1)}), bf16[16,128,512]{2,1,0:T(8,128)(2,1)S(1)}, u32[]{:S(2)}, u32[]{:S(2)}) async-start(bf16[16,128,512]{2,1,0:T(8,128)(2,1)} %copy.148), calls=%async_computation.1 | async-start | bytes 4194304 | tf_op jit(solution)/shard_map/all_to_all | solution.py:119
  22.5 1.9 convolution_convert_fusion.3
  24.4 0.7 copy-done.2
  25.1 0.8 convolution_convert_fusion.1
  25.9 2.5 %copy.138 = bf16[16,128,512]{2,1,0:T(8,128)(2,1)} copy(bf16[16,128,512]{2,0,1:T(8,128)(2,1)S(1)} %convolution_convert_fusion.1) | data formatting | bytes 4194304 | tf_op jit(solution)/shard_map/convert_element_type | solution.py:113
  28.3 35.2 %all-to-all-done.1 = bf16[16,128,512]{2,1,0:T(8,128)(2,1)S(1)} async-done(((bf16[16,128,512]{2,1,0:T(8,128)(2,1)}), bf16[16,128,512]{2,1,0:T(8,128)(2,1)S(1)}, u32[]{:S(2)}, u32[]{:S(2)}) %all-to-all-start.1) | async-done | bytes 2097184 | tf_op jit(solution)/shard_map/all_to_all | solution.py:119
  63.6 11.3 %all-to-all-start = ((bf16[16,128,512]{2,1,0:T(8,128)(2,1)}), bf16[16,128,512]{2,1,0:T(8,128)(2,1)}, u32[]{:S(2)}, u32[]{:S(2)}) async-start(bf16[16,128,512]{2,1,0:T(8,128)(2,1)} %copy.138), calls=%async_computation | async-start | bytes 4194304 | tf_op jit(solution)/shard_map/all_to_all | solution.py:118
  74.9 1.7 fusion.94
  76.6 2.9 %collective-permute-start = (bf16[128,512]{1,0:T(8,128)(2,1)}, bf16[128,512]{1,0:T(8,128)(2,1)}, u32[]{:S(2)}, u32[]{:S(2)}) collective-permute-start(bf16[128,512]{1,0:T(8,128)(2,1)} %get-tuple-element.7), channel_id=1, source_target_pairs={{0,2},{2,4},{4,6},{6,8},{8,10},{10,12},{12,14},{14,16},{16,18},{18... | collective-permute-start | bytes 393224 | tf_op jit(solution)/shard_map/ppermute | solution.py:13
  79.5 0.7 fusion.93
  80.2 3.5 %collective-permute-start.1 = (bf16[128,512]{1,0:T(8,128)(2,1)}, bf16[128,512]{1,0:T(8,128)(2,1)}, u32[]{:S(2)}, u32[]{:S(2)}) collective-permute-start(bf16[128,512]{1,0:T(8,128)(2,1)} %get-tuple-element.5), channel_id=1, source_target_pairs={{0,2},{2,4},{4,6},{6,8},{8,10},{10,12},{12,14},{14,16},{16,18},{18... | collective-permute-start | bytes 393224 | tf_op jit(solution)/shard_map/ppermute | solution.py:13
  83.8 1.7 reshape_reshape.11
  85.5 0.8 reshape_reshape.12
  86.5 2.6 %convolution_convert_fusion.4 = bf16[256,512]{1,0:T(8,128)(2,1)} fusion(bf16[1024,512]{1,0:T(8,128)(2,1)} %param.14, bf16[256,1024]{1,0:T(8,128)(2,1)} %param.12, f32[1024]{0:T(1024)S(1)} %copy-done.11, f32[256]{0:T(256)S(1)} %add_rsqrt_fusion.1), kind=kOutput, calls=%fused_computation.34 | convolution fusion | flops 269615104 | bytes 1840128 | tf_op jit(solution)/shard_map/dot_general | solution.py:84
  89.1 1.0 reshape_reshape.10
  90.1 0.7 copy.129
  90.8 0.9 concatenate.47
  91.8 0.7 copy.132
  92.4 1.0 copy.165
  93.6 0.6 copy.128
  94.2 1.3 fusion.97
  95.4 2.0 convolution_bitcast_fusion.2
  97.6 1.6 concatenate.46
  99.2 1.6 copy.131
  100.7 1.7 copy.164
  102.4 1.3 fusion.96
  103.8 2.0 convolution_bitcast_fusion.1
  105.7 1.9 gather_fusion.1
  107.6 2.6 %copy.149 = bf16[12,128,512]{1,2,0:T(8,128)(2,1)} copy(bf16[12,128,512]{2,1,0:T(8,128)(2,1)} %gather_fusion.1) | data formatting | bytes 3145728 | tf_op jit(solution)/shard_map/gather | solution.py:122
  110.2 5.8 %all-to-all-done = bf16[16,128,512]{2,1,0:T(8,128)(2,1)} async-done(((bf16[16,128,512]{2,1,0:T(8,128)(2,1)}), bf16[16,128,512]{2,1,0:T(8,128)(2,1)}, u32[]{:S(2)}, u32[]{:S(2)}) %all-to-all-start) | async-done | bytes 2097184 | tf_op jit(solution)/shard_map/all_to_all | solution.py:118
  116.0 3.4 %gather_fusion = bf16[12,128,512]{2,1,0:T(8,128)(2,1)} fusion(bf16[16,128,512]{2,1,0:T(8,128)(2,1)} %all-to-all-done, s32[1024]{0:T(1024)S(1)} %pad_clamp_fusion), kind=kCustom, calls=%fused_computation | custom fusion | bytes 3145776 | tf_op jit(solution)/shard_map/gather | solution.py:122
  119.4 1.9 copy.140
  121.4 1.3 multiply_reduce_fusion
  122.7 0.7 fusion.1
  123.4 0.7 copy-done.1
  124.1 0.7 convolution_bitcast_fusion
  125.0 0.1 copy-done.3
  125.1 0.2 copy-done.4
  125.3 0.5 fusion
  125.9 0.2 copy.153
  126.1 1.4 fusion.47
  127.6 0.1 fusion.64
  127.7 40.5 %reduce-scatter.3.cloned.1.call-done = f32[256,512]{1,0:T(8,128)} async-done(((f32[256,1024]{1,0:T(8,128)}), f32[256,512]{1,0:T(8,128)}) %reduce-scatter.3.cloned.1.call-update) | async-done | bytes 524304 | tf_op jit(solution)/shard_map/reduce_scatter | solution.py:131
  168.2 1.1 add_convert_fusion.2
  169.3 0.3 fusion.15
  169.6 0.9 copy.155
  170.5 5.6 %all-to-all-start.2 = ((bf16[2,128,512]{2,0,1:T(2,128)(2,1)}), bf16[2,128,512]{2,0,1:T(2,128)(2,1)S(1)}, u32[]{:S(2)}, u32[]{:S(2)}) async-start(bf16[2,128,512]{2,0,1:T(2,128)(2,1)} %copy.155), calls=%async_computation.3 | async-start | bytes 524288 | tf_op jit(solution)/shard_map/all_to_all | solution.py:151
  176.1 10.0 %all-to-all-done.2 = bf16[2,128,512]{2,0,1:T(2,128)(2,1)S(1)} async-done(((bf16[2,128,512]{2,0,1:T(2,128)(2,1)}), bf16[2,128,512]{2,0,1:T(2,128)(2,1)S(1)}, u32[]{:S(2)}, u32[]{:S(2)}) %all-to-all-start.2) | async-done | bytes 262176 | tf_op jit(solution)/shard_map/all_to_all | solution.py:151
  187.1 0.1 pad.39
  187.2 0.1 pad.40
  187.5 12.8 %all_to_all.28 = bf16[32,8,512]{2,1,0:T(8,128)(2,1)S(1)} all-to-all(bf16[32,8,512]{2,1,0:T(8,128)(2,1)S(1)} %add_convert_fusion.1), channel_id=1, replica_groups=mesh['tm'=16,'mp'=2] {'tm'}, dimensions={0} | all-to-all | bytes 524288 | tf_op jit(solution)/shard_map/all_to_all | solution.py:153
  200.5 8.7 %all_gather.3 = bf16[256,1024]{1,0:T(8,128)(2,1)S(1)} all-gather(bf16[256,512]{1,0:T(8,128)(2,1)S(1)} %fusion.36), channel_id=1, replica_groups=mesh['tm'=16,'mp'=2] {'mp'}, dimensions={1}, use_global_device_ids=true | all-gather | bytes 786432 | tf_op jit(solution)/shard_map/all_gather | solution.py:157
  209.3 0.2 fusion.19
  209.5 7.1 %fusion.22 = f32[256,1024]{1,0:T(8,128)} fusion(bf16[2048,1024]{1,0:T(8,128)(2,1)} %param.23, bf16[1024,2048]{1,0:T(8,128)(2,1)} %param.22, bf16[256,1024]{1,0:T(8,128)(2,1)S(1)} %all_gather.3, f32[1024]{0:T(1024)S(1)} %copy-done.12, f32[256]{0:T(256)S(1)} %add_rsqrt_fusion), kind=kOutput, calls=%fused_computation.42 | convolution fusion | flops 2153250816 | bytes 9966592 | tf_op jit(solution)/shard_map/dot_general | solution.py:163
  216.6 18.1 %reduce-scatter.5.cloned.1.call-done = f32[256,512]{1,0:T(8,128)} async-done(((f32[256,1024]{1,0:T(8,128)}), f32[256,512]{1,0:T(8,128)}) %reduce-scatter.5.cloned.1.call-update) | async-done | bytes 524304 | tf_op jit(solution)/shard_map/reduce_scatter | solution.py:162
  234.8 1.8 add_convert_fusion
  (83 shorter events, 2.3 us)
Async XLA Ops:
  6.5 119.5 %copy-start = (bf16[512,1024]{1,0:T(8,128)(2,1)S(1)}, bf16[512,1024]{1,0:T(8,128)(2,1)}, u32[]{:S(2)}) copy-start(bf16[512,1024]{1,0:T(8,128)(2,1)} %param.17) | copy-start | bytes 3145732
  15.0 7.5 %copy-start.11 = (f32[1024]{0:T(1024)S(1)}, f32[1024]{0:T(1024)}, u32[]{:S(2)}) copy-start(f32[1024]{0:T(1024)} %param.13) | copy-start | bytes 12292
  15.0 48.6 %all-to-all-start.1 = ((bf16[16,128,512]{2,1,0:T(8,128)(2,1)}), bf16[16,128,512]{2,1,0:T(8,128)(2,1)S(1)}, u32[]{:S(2)}, u32[]{:S(2)}) async-start(bf16[16,128,512]{2,1,0:T(8,128)(2,1)} %copy.148), calls=%async_computation.1 | async-start | bytes 4194304 | tf_op jit(solution)/shard_map/all_to_all | solution.py:119
  24.4 0.7 copy-start.2
  63.6 52.4 %all-to-all-start = ((bf16[16,128,512]{2,1,0:T(8,128)(2,1)}), bf16[16,128,512]{2,1,0:T(8,128)(2,1)}, u32[]{:S(2)}, u32[]{:S(2)}) async-start(bf16[16,128,512]{2,1,0:T(8,128)(2,1)} %copy.138), calls=%async_computation | async-start | bytes 4194304 | tf_op jit(solution)/shard_map/all_to_all | solution.py:118
  74.8 11.4 %copy-start.8 = (s32[32,8]{0,1:T(8,128)S(1)}, s32[32,8]{0,1:T(8,128)}, u32[]{:S(2)}) copy-start(s32[32,8]{0,1:T(8,128)} %param.18) | copy-start | bytes 3076
  74.9 93.3 %reduce-scatter.3.cloned.1.call-start = ((), (), s32[]{:S(2)}) async-start(), calls=%async_computation.6 | async-start | bytes 1572864 | tf_op jit(solution)/shard_map/reduce_scatter | solution.py:131
  76.6 21.0 %collective-permute-start = (bf16[128,512]{1,0:T(8,128)(2,1)}, bf16[128,512]{1,0:T(8,128)(2,1)}, u32[]{:S(2)}, u32[]{:S(2)}) collective-permute-start(bf16[128,512]{1,0:T(8,128)(2,1)} %get-tuple-element.7), channel_id=1, source_target_pairs={{0,2},{2,4},{4,6},{6,8},{8,10},{10,12},{12,14},{14,16},{16,18},{18... | collective-permute-start | bytes 393224 | tf_op jit(solution)/shard_map/ppermute | solution.py:13
  80.2 20.5 %collective-permute-start.1 = (bf16[128,512]{1,0:T(8,128)(2,1)}, bf16[128,512]{1,0:T(8,128)(2,1)}, u32[]{:S(2)}, u32[]{:S(2)}) collective-permute-start(bf16[128,512]{1,0:T(8,128)(2,1)} %get-tuple-element.5), channel_id=1, source_target_pairs={{0,2},{2,4},{4,6},{6,8},{8,10},{10,12},{12,14},{14,16},{16,18},{18... | collective-permute-start | bytes 393224 | tf_op jit(solution)/shard_map/ppermute | solution.py:13
  119.4 2.0 copy-start.6
  122.7 1.4 copy-start.1
  124.1 0.7 copy-start.9
  124.1 1.0 copy-start.3
  124.1 1.2 copy-start.4
  125.8 1.7 copy-start.7
  125.9 42.3 %copy-start.5 = (bf16[256,1024]{1,0:T(8,128)(2,1)S(1)}, bf16[256,1024]{1,0:T(8,128)(2,1)}, u32[]{:S(2)}) copy-start(bf16[256,1024]{1,0:T(8,128)(2,1)} %param.12) | copy-start | bytes 1572868
  127.5 48.6 %copy-start.10 = (f32[512]{0:T(512)S(1)}, f32[512]{0:T(512)}, u32[]{:S(2)}) copy-start(f32[512]{0:T(512)} %param.20) | copy-start | bytes 6148
  170.5 15.7 %all-to-all-start.2 = ((bf16[2,128,512]{2,0,1:T(2,128)(2,1)}), bf16[2,128,512]{2,0,1:T(2,128)(2,1)S(1)}, u32[]{:S(2)}, u32[]{:S(2)}) async-start(bf16[2,128,512]{2,0,1:T(2,128)(2,1)} %copy.155), calls=%async_computation.3 | async-start | bytes 524288 | tf_op jit(solution)/shard_map/all_to_all | solution.py:151
  176.1 58.7 %reduce-scatter.5.cloned.1.call-start = ((), (), s32[]{:S(2)}) async-start(), calls=%async_computation.7 | async-start | bytes 1572864 | tf_op jit(solution)/shard_map/reduce_scatter | solution.py:162
  200.3 9.1 %copy-start.12 = (f32[1024]{0:T(1024)S(1)}, f32[1024]{0:T(1024)}, u32[]{:S(2)}) copy-start(f32[1024]{0:T(1024)} %param.21) | copy-start | bytes 12292
Sparse Core Ops, SparseCore 0:
  127.7 40.4 reduce-scatter.2
  216.7 17.9 reduce-scatter.4
where the time goes:
time: 244 us; the launch traced here: 243 us
  waiting for transfers between devices  110 us (45%)
  local copies, waits for them, and re-layouts  33.6 us (14%)
  starting transfers between devices  30.9 us (13%)
  matrix products  25.2 us (10%)
  blocking collectives  21.6 us (9%)
  between operations  14 us (6%)
  other arithmetic  8.48 us (3%)
    reduce_scatter x1, waiting for transfers between devices, per_device(): lax.psum_scatter(jnp.dot(attended, output_weight, preferred_element_type=...  40.5 us
    all_to_all x1, waiting for transfers between devices, per_device(): lax.all_to_all(send_values, 'tm', split_axis=0, concat_axis=0, tiled=True)  35.2 us
    reduce_scatter x1, waiting for transfers between devices, per_device(): lax.psum_scatter(jnp.dot(hidden, down_weight, preferred_element_type=jnp....  18.1 us
    all_to_all x1, blocking collectives, per_device(): lax.all_to_all(states, 'tm', split_axis=0, concat_axis=1, tiled=True)  12.8 us
    all_to_all x1, starting transfers between devices, per_device(): lax.all_to_all(send_keys, 'tm', split_axis=0, concat_axis=0, tiled=True)  11.3 us
    all_to_all x1, waiting for transfers between devices, per_device(): lax.all_to_all(mixed, 'tm', split_axis=1, concat_axis=0, tiled=True)  9.97 us
    all_gather x1, blocking collectives, per_device(): whole = lax.all_gather(second, 'mp', axis=1, tiled=True)  8.75 us
    all_to_all x1, starting transfers between devices, per_device(): lax.all_to_all(send_values, 'tm', split_axis=0, concat_axis=0, tiled=True)  7.49 us
  transfers between devices with their start and end apart: 7, of which 5 were waited for; matrix products, arithmetic and copies ran while one was open for 14% of the time, Pallas kernels for 0%

commit v1 on v0

--- a/solution.py
+++ b/solution.py
@@ -148,7 +148,9 @@
     ).astype(jnp.bfloat16)
     retain = jnp.exp(-decay_rate)
     inject = jnp.sqrt(1.0 - retain * retain)
-    by_site = lax.all_to_all(mixed, "tm", split_axis=1, concat_axis=0, tiled=True)
+    by_site = jnp.concatenate(
+        lax.all_to_all(jnp.stack(jnp.split(mixed, lax.axis_size("tm"), axis=1)), "tm", 0, 0), axis=0
+    )
     states = running(by_site, retain, inject).astype(jnp.bfloat16)
     smoothed = lax.all_to_all(states, "tm", split_axis=0, concat_axis=1, tiled=True)
     second = (

time: 244 us -> 253 us (1.037)
  local copies, waits for them, and re-layouts: 33.6 us -> 42.4 us
    unnamed x26 -> x41, local copies, waits for them, and re-layouts: 1.75 us -> 10.8 us
where the time goes in v1:
time: 253 us; the launch traced here: 252 us
  waiting for transfers between devices  110 us (43%)
  local copies, waits for them, and re-layouts  42.4 us (17%)
  starting transfers between devices  30.9 us (12%)
  matrix products  25.2 us (10%)
  blocking collectives  21.6 us (9%)
  between operations  14 us (6%)
  other arithmetic  8.43 us (3%)
    reduce_scatter x1, waiting for transfers between devices, per_device(): lax.psum_scatter(jnp.dot(attended, output_weight, preferred_element_type=...  40.5 us
    all_to_all x1, waiting for transfers between devices, per_device(): lax.all_to_all(send_values, 'tm', split_axis=0, concat_axis=0, tiled=True)  35.2 us
    reduce_scatter x1, waiting for transfers between devices, per_device(): lax.psum_scatter(jnp.dot(hidden, down_weight, preferred_element_type=jnp....  18.1 us
    all_to_all x1, blocking collectives, per_device(): lax.all_to_all(states, 'tm', split_axis=0, concat_axis=1, tiled=True)  12.8 us
    all_to_all x1, starting transfers between devices, per_device(): lax.all_to_all(send_keys, 'tm', split_axis=0, concat_axis=0, tiled=True)  11.3 us
    unnamed x41, local copies, waits for them, and re-layouts  10.8 us
    all_to_all x1, waiting for transfers between devices, per_device(): lax.all_to_all(jnp.stack(jnp.split(mixed, lax.axis_size('tm'), axis=1)),...  9.97 us
    all_gather x1, blocking collectives, per_device(): whole = lax.all_gather(second, 'mp', axis=1, tiled=True)  8.75 us
  transfers between devices with their start and end apart: 7, of which 5 were waited for; matrix products, arithmetic and copies ran while one was open for 14% of the time, Pallas kernels for 0%

profile of v1, /device:TPU:0, one launch (start us, length us, event | category | flops | bytes accessed | tf_op | source)
XLA Modules:
  0.0 252.1 jit_solution(14939175065498012190)
XLA Ops:
  6.5 1.3 fusion.16
  7.9 0.7 slice_compare_fusion
  8.6 0.7 slice_subtract_fusion
  9.7 1.9 convolution_convert_fusion.2
  11.6 0.8 convolution_convert_fusion
  12.4 2.5 copy.136
  15.0 7.5 %all-to-all-start.1 = ((bf16[16,128,512]{2,1,0:T(8,128)(2,1)}), bf16[16,128,512]{2,1,0:T(8,128)(2,1)S(1)}, u32[]{:S(2)}, u32[]{:S(2)}) async-start(bf16[16,128,512]{2,1,0:T(8,128)(2,1)} %copy.136), calls=%async_computation.1 | async-start | bytes 4194304 | tf_op jit(solution)/shard_map/all_to_all | solution.py:119
  22.5 1.9 convolution_convert_fusion.3
  24.4 0.7 copy-done.2
  25.1 0.8 convolution_convert_fusion.1
  25.9 2.5 copy.126
  28.3 35.2 %all-to-all-done.1 = bf16[16,128,512]{2,1,0:T(8,128)(2,1)S(1)} async-done(((bf16[16,128,512]{2,1,0:T(8,128)(2,1)}), bf16[16,128,512]{2,1,0:T(8,128)(2,1)S(1)}, u32[]{:S(2)}, u32[]{:S(2)}) %all-to-all-start.1) | async-done | bytes 2097184 | tf_op jit(solution)/shard_map/all_to_all | solution.py:119
  63.6 11.3 %all-to-all-start = ((bf16[16,128,512]{2,1,0:T(8,128)(2,1)}), bf16[16,128,512]{2,1,0:T(8,128)(2,1)}, u32[]{:S(2)}, u32[]{:S(2)}) async-start(bf16[16,128,512]{2,1,0:T(8,128)(2,1)} %copy.126), calls=%async_computation | async-start | bytes 4194304 | tf_op jit(solution)/shard_map/all_to_all | solution.py:118
  74.9 1.7 fusion.94
  76.6 2.9 %collective-permute-start = (bf16[128,512]{1,0:T(8,128)(2,1)}, bf16[128,512]{1,0:T(8,128)(2,1)}, u32[]{:S(2)}, u32[]{:S(2)}) collective-permute-start(bf16[128,512]{1,0:T(8,128)(2,1)} %get-tuple-element.7), channel_id=1, source_target_pairs={{0,2},{2,4},{4,6},{6,8},{8,10},{10,12},{12,14},{14,16},{16,18},{18... | collective-permute-start | bytes 393224 | tf_op jit(solution)/shard_map/ppermute | solution.py:13
  79.5 0.7 fusion.93
  80.2 3.5 %collective-permute-start.1 = (bf16[128,512]{1,0:T(8,128)(2,1)}, bf16[128,512]{1,0:T(8,128)(2,1)}, u32[]{:S(2)}, u32[]{:S(2)}) collective-permute-start(bf16[128,512]{1,0:T(8,128)(2,1)} %get-tuple-element.5), channel_id=1, source_target_pairs={{0,2},{2,4},{4,6},{6,8},{8,10},{10,12},{12,14},{14,16},{16,18},{18... | collective-permute-start | bytes 393224 | tf_op jit(solution)/shard_map/ppermute | solution.py:13
  83.8 1.7 reshape_reshape.11
  85.5 0.8 reshape_reshape.12
  86.5 2.6 %convolution_convert_fusion.4 = bf16[256,512]{1,0:T(8,128)(2,1)} fusion(bf16[1024,512]{1,0:T(8,128)(2,1)} %param.14, bf16[256,1024]{1,0:T(8,128)(2,1)} %param.12, f32[1024]{0:T(1024)S(1)} %copy-done.11, f32[256]{0:T(256)S(1)} %add_rsqrt_fusion.1), kind=kOutput, calls=%fused_computation.34 | convolution fusion | flops 269615104 | bytes 1840128 | tf_op jit(solution)/shard_map/dot_general | solution.py:84
  89.1 1.0 reshape_reshape.10
  90.1 0.7 copy.117
  90.8 0.9 concatenate.47
  91.8 0.7 copy.120
  92.4 1.0 copy.148
  94.2 1.3 fusion.97
  95.4 2.0 convolution_bitcast_fusion.2
  97.6 1.6 concatenate.46
  99.2 1.6 copy.119
  100.7 1.7 copy.147
  102.4 1.3 fusion.96
  103.8 2.0 convolution_bitcast_fusion.1
  105.7 1.9 gather_fusion.1
  107.6 2.6 %copy.137 = bf16[12,128,512]{1,2,0:T(8,128)(2,1)} copy(bf16[12,128,512]{2,1,0:T(8,128)(2,1)} %gather_fusion.1) | data formatting | bytes 3145728 | tf_op jit(solution)/shard_map/gather | solution.py:122
  110.2 5.8 %all-to-all-done = bf16[16,128,512]{2,1,0:T(8,128)(2,1)} async-done(((bf16[16,128,512]{2,1,0:T(8,128)(2,1)}), bf16[16,128,512]{2,1,0:T(8,128)(2,1)}, u32[]{:S(2)}, u32[]{:S(2)}) %all-to-all-start) | async-done | bytes 2097184 | tf_op jit(solution)/shard_map/all_to_all | solution.py:118
  116.0 3.4 %gather_fusion = bf16[12,128,512]{2,1,0:T(8,128)(2,1)} fusion(bf16[16,128,512]{2,1,0:T(8,128)(2,1)} %all-to-all-done, s32[1024]{0:T(1024)S(1)} %pad_clamp_fusion), kind=kCustom, calls=%fused_computation | custom fusion | bytes 3145776 | tf_op jit(solution)/shard_map/gather | solution.py:122
  119.4 1.9 copy.128
  121.4 1.3 multiply_reduce_fusion
  122.7 0.7 fusion.1
  123.4 0.7 copy-done.1
  124.1 0.7 convolution_bitcast_fusion
  126.1 1.4 fusion.47
  127.7 40.5 %reduce-scatter.3.cloned.1.call-done = f32[256,512]{1,0:T(8,128)} async-done(((f32[256,1024]{1,0:T(8,128)}), f32[256,512]{1,0:T(8,128)}) %reduce-scatter.3.cloned.1.call-update) | async-done | bytes 524304 | tf_op jit(solution)/shard_map/reduce_scatter | solution.py:131
  168.2 1.1 add_convert_fusion.2
  169.5 0.6 constant_dynamic-update-slice_fusion.15
  170.1 0.6 constant_dynamic-update-slice_fusion.14
  170.7 0.6 constant_dynamic-update-slice_fusion.13
  171.3 0.6 constant_dynamic-update-slice_fusion.12
  172.6 0.6 constant_dynamic-update-slice_fusion.10
  173.2 0.6 constant_dynamic-update-slice_fusion.9
  173.8 0.6 constant_dynamic-update-slice_fusion.8
  174.4 0.6 constant_dynamic-update-slice_fusion.7
  175.0 0.6 constant_dynamic-update-slice_fusion.6
  175.6 0.6 constant_dynamic-update-slice_fusion.5
  176.2 0.6 constant_dynamic-update-slice_fusion.4
  178.0 0.6 constant_dynamic-update-slice_fusion.1
  178.6 0.6 constant_dynamic-update-slice_fusion
  179.2 5.6 %all-to-all-start.2 = ((bf16[16,2,8,512]{3,2,1,0:T(8,128)(2,1)}), bf16[16,2,8,512]{3,2,1,0:T(8,128)(2,1)S(1)}, u32[]{:S(2)}, u32[]{:S(2)}) async-start(bf16[16,2,8,512]{3,2,1,0:T(8,128)(2,1)} %constant_dynamic-update-slice_fusion), calls=%async_computation.3 | async-start | bytes 524288 | tf_op jit(solution)/shard_map/all_to_all | solution.py:152
  184.9 10.0 %all-to-all-done.2 = bf16[16,2,8,512]{3,2,1,0:T(8,128)(2,1)S(1)} async-done(((bf16[16,2,8,512]{3,2,1,0:T(8,128)(2,1)}), bf16[16,2,8,512]{3,2,1,0:T(8,128)(2,1)S(1)}, u32[]{:S(2)}, u32[]{:S(2)}) %all-to-all-start.2) | async-done | bytes 262176 | tf_op jit(solution)/shard_map/all_to_all | solution.py:152
  196.2 12.8 %all_to_all.24 = bf16[32,8,512]{2,1,0:T(8,128)(2,1)S(1)} all-to-all(bf16[32,8,512]{2,1,0:T(8,128)(2,1)S(1)} %add_convert_fusion.1), channel_id=1, replica_groups=mesh['tm'=16,'mp'=2] {'tm'}, dimensions={0} | all-to-all | bytes 524288 | tf_op jit(solution)/shard_map/all_to_all | solution.py:155
  209.2 8.7 %all_gather.3 = bf16[256,1024]{1,0:T(8,128)(2,1)S(1)} all-gather(bf16[256,512]{1,0:T(8,128)(2,1)S(1)} %fusion.36), channel_id=1, replica_groups=mesh['tm'=16,'mp'=2] {'mp'}, dimensions={1}, use_global_device_ids=true | all-gather | bytes 786432 | tf_op jit(solution)/shard_map/all_gather | solution.py:159
  218.1 7.1 %fusion.22 = f32[256,1024]{1,0:T(8,128)} fusion(bf16[2048,1024]{1,0:T(8,128)(2,1)} %param.23, bf16[1024,2048]{1,0:T(8,128)(2,1)} %param.22, bf16[256,1024]{1,0:T(8,128)(2,1)S(1)} %all_gather.3, f32[1024]{0:T(1024)S(1)} %copy-done.12, f32[256]{0:T(256)S(1)} %add_rsqrt_fusion), kind=kOutput, calls=%fused_computation.42 | convolution fusion | flops 2153250816 | bytes 9966592 | tf_op jit(solution)/shard_map/dot_general | solution.py:165
  225.3 18.1 %reduce-scatter.5.cloned.1.call-done = f32[256,512]{1,0:T(8,128)} async-done(((f32[256,1024]{1,0:T(8,128)}), f32[256,512]{1,0:T(8,128)}) %reduce-scatter.5.cloned.1.call-update) | async-done | bytes 524304 | tf_op jit(solution)/shard_map/reduce_scatter | solution.py:164
  243.4 1.8 add_convert_fusion
  (96 shorter events, 6.6 us)
Async XLA Ops:
  6.5 119.5 %copy-start = (bf16[512,1024]{1,0:T(8,128)(2,1)S(1)}, bf16[512,1024]{1,0:T(8,128)(2,1)}, u32[]{:S(2)}) copy-start(bf16[512,1024]{1,0:T(8,128)(2,1)} %param.17) | copy-start | bytes 3145732
  15.0 7.5 %copy-start.11 = (f32[1024]{0:T(1024)S(1)}, f32[1024]{0:T(1024)}, u32[]{:S(2)}) copy-start(f32[1024]{0:T(1024)} %param.13) | copy-start | bytes 12292
  15.0 48.6 %all-to-all-start.1 = ((bf16[16,128,512]{2,1,0:T(8,128)(2,1)}), bf16[16,128,512]{2,1,0:T(8,128)(2,1)S(1)}, u32[]{:S(2)}, u32[]{:S(2)}) async-start(bf16[16,128,512]{2,1,0:T(8,128)(2,1)} %copy.136), calls=%async_computation.1 | async-start | bytes 4194304 | tf_op jit(solution)/shard_map/all_to_all | solution.py:119
  24.4 0.7 copy-start.2
  63.6 52.4 %all-to-all-start = ((bf16[16,128,512]{2,1,0:T(8,128)(2,1)}), bf16[16,128,512]{2,1,0:T(8,128)(2,1)}, u32[]{:S(2)}, u32[]{:S(2)}) async-start(bf16[16,128,512]{2,1,0:T(8,128)(2,1)} %copy.126), calls=%async_computation | async-start | bytes 4194304 | tf_op jit(solution)/shard_map/all_to_all | solution.py:118
  74.8 11.4 %copy-start.8 = (s32[32,8]{0,1:T(8,128)S(1)}, s32[32,8]{0,1:T(8,128)}, u32[]{:S(2)}) copy-start(s32[32,8]{0,1:T(8,128)} %param.18) | copy-start | bytes 3076
  74.9 93.3 %reduce-scatter.3.cloned.1.call-start = ((), (), s32[]{:S(2)}) async-start(), calls=%async_computation.6 | async-start | bytes 1572864 | tf_op jit(solution)/shard_map/reduce_scatter | solution.py:131
  76.6 21.0 %collective-permute-start = (bf16[128,512]{1,0:T(8,128)(2,1)}, bf16[128,512]{1,0:T(8,128)(2,1)}, u32[]{:S(2)}, u32[]{:S(2)}) collective-permute-start(bf16[128,512]{1,0:T(8,128)(2,1)} %get-tuple-element.7), channel_id=1, source_target_pairs={{0,2},{2,4},{4,6},{6,8},{8,10},{10,12},{12,14},{14,16},{16,18},{18... | collective-permute-start | bytes 393224 | tf_op jit(solution)/shard_map/ppermute | solution.py:13
  80.2 20.5 %collective-permute-start.1 = (bf16[128,512]{1,0:T(8,128)(2,1)}, bf16[128,512]{1,0:T(8,128)(2,1)}, u32[]{:S(2)}, u32[]{:S(2)}) collective-permute-start(bf16[128,512]{1,0:T(8,128)(2,1)} %get-tuple-element.5), channel_id=1, source_target_pairs={{0,2},{2,4},{4,6},{6,8},{8,10},{10,12},{12,14},{14,16},{16,18},{18... | collective-permute-start | bytes 393224 | tf_op jit(solution)/shard_map/ppermute | solution.py:13
  119.4 2.0 copy-start.6
  122.7 1.4 copy-start.1
  124.1 0.7 copy-start.9
  124.1 1.0 copy-start.3
  124.1 1.2 copy-start.4
  125.8 1.7 copy-start.7
  125.9 42.3 %copy-start.5 = (bf16[256,1024]{1,0:T(8,128)(2,1)S(1)}, bf16[256,1024]{1,0:T(8,128)(2,1)}, u32[]{:S(2)}) copy-start(bf16[256,1024]{1,0:T(8,128)(2,1)} %param.12) | copy-start | bytes 1572868
  127.5 57.4 %copy-start.10 = (f32[512]{0:T(512)S(1)}, f32[512]{0:T(512)}, u32[]{:S(2)}) copy-start(f32[512]{0:T(512)} %param.20) | copy-start | bytes 6148
  179.2 15.7 %all-to-all-start.2 = ((bf16[16,2,8,512]{3,2,1,0:T(8,128)(2,1)}), bf16[16,2,8,512]{3,2,1,0:T(8,128)(2,1)S(1)}, u32[]{:S(2)}, u32[]{:S(2)}) async-start(bf16[16,2,8,512]{3,2,1,0:T(8,128)(2,1)} %constant_dynamic-update-slice_fusion), calls=%async_computation.3 | async-start | bytes 524288 | tf_op jit(solution)/shard_map/all_to_all | solution.py:152
  184.8 58.6 %reduce-scatter.5.cloned.1.call-start = ((), (), s32[]{:S(2)}) async-start(), calls=%async_computation.7 | async-start | bytes 1572864 | tf_op jit(solution)/shard_map/reduce_scatter | solution.py:164
  209.0 9.1 %copy-start.12 = (f32[1024]{0:T(1024)S(1)}, f32[1024]{0:T(1024)}, u32[]{:S(2)}) copy-start(f32[1024]{0:T(1024)} %param.21) | copy-start | bytes 12292
Sparse Core Ops, SparseCore 0:
  127.7 40.4 reduce-scatter.2
  225.4 17.9 reduce-scatter.4
